TPU v7x, 128 devices: a whole 4x4x4 slice. The times are simulated.
128 devices in a mesh: grp: 32 (over y, x, core), blk: 4 (over z).
Axes of the slice: x: 4, y: 4, z: 4, core: 2. Of those that a mesh axis runs over, the one named last changes fastest.
Arguments:
- embeddings: bfloat16 [131072, 1024], P(('grp', 'blk')), may hold values from -6 to 6
- doc_group: int32 [131072, 1], P(('grp', 'blk')), may hold values from 0 to 31; in each aligned block of 1024 rows (0 to 1023, 1024 to 2047, ...) at most 48 rows name the same one
- doc_cluster: int32 [131072], P(('grp', 'blk')), may hold values from 0 to 1
Outputs:
- max_sim: float32 [131072], P(('grp', 'blk'))
Inputs may be any that keep to these rules, and one draw needn't show every extreme that they name: `doc_group`: in each aligned block of 1024 rows (the rows of one device) no subgroup is named by more than 48 rows, a bound that some block reaches.
All inputs are finite; a program needn't handle non-finite values.
Results may differ from a plain program's by a relative error of at most 0.0013.
Values may be sent and summed in bfloat16 or wider, within the bound.
A program may use at most 64 MiB of HBM per device.

v0:
```python
import jax
import jax.numpy as jnp
from jax import lax
from jax.sharding import PartitionSpec as P

RECV = 1536


def shifted(x, axis, by):
    devices = lax.axis_size(axis)
    return lax.ppermute(x, axis, [(i, (i + by) % devices) for i in range(devices)])


def tile_scores(rows, row_labels, cols, col_labels, row_start, col_start):
    count = rows.shape[0]
    total = cols.shape[0]
    row_pos = row_start + jnp.arange(count, dtype=jnp.int32)
    row_best = jnp.full((count,), -1.0, jnp.float32)
    for begin in range(0, total, 512):
        finish = min(total, begin + 512)
        sims = lax.dot_general(
            rows, cols[begin:finish], (((1,), (1,)), ((), ())), preferred_element_type=jnp.float32
        )
        col_pos = col_start + begin + jnp.arange(finish - begin, dtype=jnp.int32)
        mask = (row_labels[:, None] == col_labels[begin:finish][None, :]) & (
            row_pos[:, None] != col_pos[None, :]
        )
        masked = jnp.where(mask, sims, jnp.float32(-1.0))
        row_best = jnp.maximum(row_best, jnp.max(masked, axis=1))
    return (row_best, row_best)


def per_device(embeddings, doc_group, doc_cluster):
    groups = lax.axis_size("grp")
    blocks = lax.axis_size("blk")
    width = embeddings.shape[1]
    capacity = RECV // groups
    values = embeddings.astype(jnp.float32)
    unit = (values / jnp.sqrt(jnp.sum(values * values, axis=1, keepdims=True) + 1e-06)).astype(
        jnp.bfloat16
    )
    target = doc_group[:, 0]
    onehot = (target[:, None] == jnp.arange(groups, dtype=jnp.int32)[None, :]).astype(jnp.int32)
    rank = jnp.sum((jnp.cumsum(onehot, axis=0) - 1) * onehot, axis=1)
    slot = target * capacity + rank
    outgoing = jnp.zeros((groups * capacity, width), jnp.bfloat16).at[slot].set(unit)
    out_labels = (
        jnp.full((groups * capacity,), -1.0, jnp.bfloat16)
        .at[slot]
        .set(doc_cluster.astype(jnp.bfloat16))
    )
    held, held_labels = (
        lax.all_to_all(outgoing, "grp", split_axis=0, concat_axis=0, tiled=True),
        lax.all_to_all(out_labels, "grp", split_axis=0, concat_axis=0, tiled=True),
    )
    count = held.shape[0]
    mine = lax.axis_index("blk") * count
    best, unused = tile_scores(held, held_labels, held, held_labels, mine, mine)
    moving = (held, held_labels)
    for step in range(1, blocks):
        moving = shifted((moving[0], moving[1]), "blk", 1)
        source = (lax.axis_index("blk") - step) % blocks * count
        found, unused = tile_scores(held, held_labels, moving[0], moving[1], mine, source)
        best = jnp.maximum(best, found)
    answers = lax.all_to_all(best, "grp", split_axis=0, concat_axis=0, tiled=True)
    return answers[slot]


def solution(mesh):
    in_specs = (P(("grp", "blk"), None), P(("grp", "blk"), None), P(("grp", "blk")))
    out_specs = P(("grp", "blk"))
    return jax.shard_map(
        per_device, mesh=mesh, in_specs=in_specs, out_specs=out_specs, check_vma=False
    )
```

profile of v0, /device:TPU:1, one launch (start us, length us, event | category | flops | bytes accessed | tf_op | source)
XLA Modules:
  0.0 337.4 jit_solution(2237544170533780372)
XLA Ops:
  0.0 2.1 fusion
  2.1 0.7 fusion.50
  2.8 9.0 %reduce-window.6 = s32[32,8,128]{2,1,0:T(8,128)S(1)} reduce-window(s32[32,8,128]{2,1,0:T(8,128)S(1)} %fusion.50, s32[]{:T(128)} %constant.49.clone.1), window={size=1x1x128 pad=0_0x0_0x127_0}, to_apply=%region_0.0 | reduce-window | flops 4161536 | bytes 262148 | tf_op jit(solution)/shard_map/reduce-window
  12.3 7.3 %scatter_custom_fusion.1 = bf16[1536,1024]{1,0:T(8,128)(2,1)S(1)} fusion(s32[1024]{0:T(1024)S(1)} %bitcast.42, bf16[1024,1024]{1,0:T(8,128)(2,1)} %param.3, f32[1024]{0:T(1024)S(1)} %add_sqrt_fusion, bf16[]{:T(256)} %constant.53.clone.1), kind=kCustom, calls=%fused_computation.19 | custom fusion | flops 3145728 | bytes 5246978 | tf_op jit(solution)/shard_map/scatter | solution.py:46
  19.7 48.1 %all_to_all.31 = bf16[32,48,1024]{2,1,0:T(8,128)(2,1)} all-to-all(bf16[32,48,1024]{2,1,0:T(8,128)(2,1)S(1)} %bitcast.36), channel_id=1, replica_groups=mesh['grp'=32,'blk'=4] {'grp'}, dimensions={0} | all-to-all | bytes 6291456 | tf_op jit(solution)/shard_map/all_to_all | solution.py:53
  67.8 1.6 collective-permute-start.1
  69.5 7.6 %scatter_custom_fusion = bf16[1536]{0:T(1024)(128)(2,1)S(1)} fusion(s32[1024]{0:T(1024)S(1)} %bitcast.43, bf16[1024]{0:T(1024)(128)(2,1)S(1)} %convert_element_type.15, bf16[]{:T(256)} %constant.24.clone.1), kind=kCustom, calls=%fused_computation.70 | custom fusion | bytes 3074 | tf_op jit(solution)/shard_map/scatter | solution.py:50
  77.0 0.7 all_to_all.27
  77.7 4.2 %all-to-all-start = ((bf16[32,48,1]{1,2,0:T(2,128)(2,1)}), bf16[32,48,1]{1,2,0:T(2,128)(2,1)S(1)}, u32[]{:S(2)}, u32[]{:S(2)}) async-start(bf16[32,48,1]{1,2,0:T(2,128)(2,1)} %all_to_all.27), calls=%async_computation | async-start | bytes 32768 | tf_op jit(solution)/shard_map/all_to_all | solution.py:54
  82.0 58.0 %collective-permute-done.1 = bf16[1536,1024]{1,0:T(8,128)(2,1)} collective-permute-done((bf16[1536,1024]{1,0:T(8,128)(2,1)}, bf16[1536,1024]{1,0:T(8,128)(2,1)}, u32[]{:S(2)}, u32[]{:S(2)}) %collective-permute-start.1) | collective-permute-done | bytes 3145760 | tf_op jit(solution)/shard_map/ppermute | solution.py:11
  140.2 0.7 collective-permute-start
  140.9 69.4 %collective-permute-done = bf16[1536]{0:T(1024)(128)(2,1)S(1)} collective-permute-done((bf16[1536]{0:T(1024)(128)(2,1)S(1)}, bf16[1536]{0:T(1024)(128)(2,1)S(1)}, u32[]{:S(2)}, u32[]{:S(2)}) %collective-permute-start) | collective-permute-done | bytes 3104 | tf_op jit(solution)/shard_map/ppermute | solution.py:11
  210.3 3.7 %collective-permute-done.2 = bf16[1536]{0:T(1024)(128)(2,1)S(1)} collective-permute-done((bf16[1536]{0:T(1024)(128)(2,1)S(1)}, bf16[1536]{0:T(1024)(128)(2,1)S(1)}, u32[]{:S(2)}, u32[]{:S(2)}) %collective-permute-start.2) | collective-permute-done | bytes 3104 | tf_op jit(solution)/shard_map/ppermute | solution.py:11
  214.0 3.7 %collective-permute-done.4 = bf16[1536]{0:T(1024)(128)(2,1)S(1)} collective-permute-done((bf16[1536]{0:T(1024)(128)(2,1)S(1)}, bf16[1536]{0:T(1024)(128)(2,1)S(1)}, u32[]{:S(2)}, u32[]{:S(2)}) %collective-permute-start.4) | collective-permute-done | bytes 3104 | tf_op jit(solution)/shard_map/ppermute | solution.py:11
  217.7 4.1 %fusion.8 = f32[1536]{0:T(1024)S(1)} fusion(bf16[1536,1024]{1,0:T(8,128)(2,1)} %bitcast.7, s32[512]{0:T(512)S(1)} %iota_add_fusion.10, s32[1536]{0:T(1024)S(1)} %iota_add_fusion, bf16[1536]{0:T(1024)(128)(2,1)S(1)} %eq.82, bf16[512]{0:T(512)(128)(2,1)S(1)} %get-tuple-element.6), kind=kOutput, calls=%fused_computation.24 | convolution fusion | flops 1616116224 | bytes 4212736 | tf_op jit(solution)/shard_map/dot_general | solution.py:21
  221.8 4.1 %fusion.7 = f32[1536]{0:T(1024)S(1)} fusion(bf16[1536,1024]{1,0:T(8,128)(2,1)} %bitcast.7, s32[512]{0:T(512)S(1)} %iota_add_fusion.11, s32[1536]{0:T(1024)S(1)} %iota_add_fusion, bf16[1536]{0:T(1024)(128)(2,1)S(1)} %eq.82, bf16[512]{0:T(512)(128)(2,1)S(1)} %get-tuple-element.7), kind=kOutput, calls=%fused_computation.23 | convolution fusion | flops 1616116224 | bytes 4212736 | tf_op jit(solution)/shard_map/dot_general | solution.py:21
  225.9 4.1 %fusion.6 = f32[1536]{0:T(1024)S(1)} fusion(bf16[1536,1024]{1,0:T(8,128)(2,1)} %bitcast.7, s32[512]{0:T(512)S(1)} %iota_add_fusion.12, s32[1536]{0:T(1024)S(1)} %iota_add_fusion, bf16[1536]{0:T(1024)(128)(2,1)S(1)} %eq.82, bf16[512]{0:T(512)(128)(2,1)S(1)} %get-tuple-element.5), kind=kOutput, calls=%fused_computation.22 | convolution fusion | flops 1616116224 | bytes 4212736 | tf_op jit(solution)/shard_map/dot_general | solution.py:21
  230.1 4.1 %select_reduce_fusion.6 = f32[1536]{0:T(1024)S(1)} fusion(s32[1536]{0:T(1024)S(1)} %iota_add_fusion, s32[512]{0:T(512)S(1)} %iota_add_fusion.7, bf16[1536,1024]{1,0:T(8,128)(2,1)} %bitcast.7, bf16[1536,1024]{1,0:T(8,128)(2,1)} %collective-permute-done.1, bf16[1536]{0:T(1024)(128)(2,1)S(1)} %eq.82, bf16[512]{0:T(512)(128)(2,1)S(1)} %get-tuple-element.9), kind=kOutput, calls=%fused_computation.16 | convolution fusion | flops 1616116224 | bytes 4212736 | tf_op jit(solution)/shard_map/dot_general | solution.py:21
  234.3 4.1 %select_reduce_fusion.7 = f32[1536]{0:T(1024)S(1)} fusion(s32[1536]{0:T(1024)S(1)} %iota_add_fusion, s32[512]{0:T(512)S(1)} %iota_add_fusion.8, bf16[1536,1024]{1,0:T(8,128)(2,1)} %bitcast.7, bf16[1536,1024]{1,0:T(8,128)(2,1)} %collective-permute-done.1, bf16[1536]{0:T(1024)(128)(2,1)S(1)} %eq.82, bf16[512]{0:T(512)(128)(2,1)S(1)} %get-tuple-element.10), kind=kOutput, calls=%fused_computation.17 | convolution fusion | flops 1616116224 | bytes 4212736 | tf_op jit(solution)/shard_map/dot_general | solution.py:21
  238.4 4.1 %select_reduce_fusion.8 = f32[1536]{0:T(1024)S(1)} fusion(s32[1536]{0:T(1024)S(1)} %iota_add_fusion, s32[512]{0:T(512)S(1)} %iota_add_fusion.9, bf16[1536,1024]{1,0:T(8,128)(2,1)} %bitcast.7, bf16[1536,1024]{1,0:T(8,128)(2,1)} %collective-permute-done.1, bf16[1536]{0:T(1024)(128)(2,1)S(1)} %eq.82, bf16[512]{0:T(512)(128)(2,1)S(1)} %get-tuple-element.8), kind=kOutput, calls=%fused_computation.18 | convolution fusion | flops 1616116224 | bytes 4212736 | tf_op jit(solution)/shard_map/dot_general | solution.py:21
  242.5 4.1 %select_reduce_fusion.3 = f32[1536]{0:T(1024)S(1)} fusion(s32[1536]{0:T(1024)S(1)} %iota_add_fusion, s32[512]{0:T(512)S(1)} %iota_add_fusion.4, bf16[1536,1024]{1,0:T(8,128)(2,1)} %bitcast.7, bf16[1536,1024]{1,0:T(8,128)(2,1)} %collective-permute-done.3, bf16[1536]{0:T(1024)(128)(2,1)S(1)} %eq.82, bf16[512]{0:T(512)(128)(2,1)S(1)} %get-tuple-element.12), kind=kOutput, calls=%fused_computation.13 | convolution fusion | flops 1616116224 | bytes 4212736 | tf_op jit(solution)/shard_map/dot_general | solution.py:21
  246.6 4.1 %select_reduce_fusion.4 = f32[1536]{0:T(1024)S(1)} fusion(s32[1536]{0:T(1024)S(1)} %iota_add_fusion, s32[512]{0:T(512)S(1)} %iota_add_fusion.5, bf16[1536,1024]{1,0:T(8,128)(2,1)} %bitcast.7, bf16[1536,1024]{1,0:T(8,128)(2,1)} %collective-permute-done.3, bf16[1536]{0:T(1024)(128)(2,1)S(1)} %eq.82, bf16[512]{0:T(512)(128)(2,1)S(1)} %get-tuple-element.13), kind=kOutput, calls=%fused_computation.14 | convolution fusion | flops 1616116224 | bytes 4212736 | tf_op jit(solution)/shard_map/dot_general | solution.py:21
  250.8 4.1 %select_reduce_fusion.5 = f32[1536]{0:T(1024)S(1)} fusion(s32[1536]{0:T(1024)S(1)} %iota_add_fusion, s32[512]{0:T(512)S(1)} %iota_add_fusion.6, bf16[1536,1024]{1,0:T(8,128)(2,1)} %bitcast.7, bf16[1536,1024]{1,0:T(8,128)(2,1)} %collective-permute-done.3, bf16[1536]{0:T(1024)(128)(2,1)S(1)} %eq.82, bf16[512]{0:T(512)(128)(2,1)S(1)} %get-tuple-element.11), kind=kOutput, calls=%fused_computation.15 | convolution fusion | flops 1616116224 | bytes 4212736 | tf_op jit(solution)/shard_map/dot_general | solution.py:21
  254.9 42.2 %collective-permute-done.5 = bf16[1536,1024]{1,0:T(8,128)(2,1)S(1)} collective-permute-done((bf16[1536,1024]{1,0:T(8,128)(2,1)}, bf16[1536,1024]{1,0:T(8,128)(2,1)S(1)}, u32[]{:S(2)}, u32[]{:S(2)}) %collective-permute-start.5) | collective-permute-done | bytes 3145760 | tf_op jit(solution)/shard_map/ppermute | solution.py:11
  297.1 3.8 %select_reduce_fusion = f32[1536]{0:T(1024)S(1)} fusion(s32[1536]{0:T(1024)S(1)} %iota_add_fusion, s32[512]{0:T(512)S(1)} %iota_add_fusion.1, bf16[1536,1024]{1,0:T(8,128)(2,1)} %bitcast.7, bf16[1536,1024]{1,0:T(8,128)(2,1)S(1)} %collective-permute-done.5, bf16[1536]{0:T(1024)(128)(2,1)S(1)} %eq.82, bf16[512]{0:T(512)(128)(2,1)S(1)} %get-tuple-element.15), kind=kOutput, calls=%fused_computation.10 | convolution fusion | flops 1616116224 | bytes 4215808 | tf_op jit(solution)/shard_map/dot_general | solution.py:21
  300.9 4.1 %select_reduce_fusion.1 = f32[1536]{0:T(1024)S(1)} fusion(s32[1536]{0:T(1024)S(1)} %iota_add_fusion, s32[512]{0:T(512)S(1)} %iota_add_fusion.2, bf16[1536,1024]{1,0:T(8,128)(2,1)} %bitcast.7, bf16[1536,1024]{1,0:T(8,128)(2,1)S(1)} %collective-permute-done.5, bf16[1536]{0:T(1024)(128)(2,1)S(1)} %eq.82, bf16[512]{0:T(512)(128)(2,1)S(1)} %get-tuple-element.16), kind=kOutput, calls=%fused_computation.11 | convolution fusion | flops 1616116224 | bytes 4215808 | tf_op jit(solution)/shard_map/dot_general | solution.py:21
  305.0 3.8 %select_reduce_fusion.2 = f32[1536]{0:T(1024)S(1)} fusion(s32[1536]{0:T(1024)S(1)} %iota_add_fusion, s32[512]{0:T(512)S(1)} %iota_add_fusion.3, bf16[1536,1024]{1,0:T(8,128)(2,1)} %bitcast.7, bf16[1536,1024]{1,0:T(8,128)(2,1)S(1)} %collective-permute-done.5, bf16[1536]{0:T(1024)(128)(2,1)S(1)} %eq.82, bf16[512]{0:T(512)(128)(2,1)S(1)} %get-tuple-element.14), kind=kOutput, calls=%fused_computation.12 | convolution fusion | flops 1616116224 | bytes 4215808 | tf_op jit(solution)/shard_map/dot_general | solution.py:21
  308.9 0.7 reshape.245
  309.5 9.1 %all-to-all-start.2 = ((f32[32,48,1]{1,2,0:T(1,128)}), f32[32,48,1]{1,2,0:T(1,128)S(1)}, u32[]{:S(2)}, u32[]{:S(2)}) async-start(f32[32,48,1]{1,2,0:T(1,128)} %bitcast.8), calls=%async_computation.2 | async-start | bytes 32768 | tf_op jit(solution)/shard_map/all_to_all | solution.py:65
  318.7 6.9 %all-to-all-done.2 = f32[32,48,1]{1,2,0:T(1,128)S(1)} async-done(((f32[32,48,1]{1,2,0:T(1,128)}), f32[32,48,1]{1,2,0:T(1,128)S(1)}, u32[]{:S(2)}, u32[]{:S(2)}) %all-to-all-start.2) | async-done | bytes 6176 | tf_op jit(solution)/shard_map/all_to_all | solution.py:65
  326.1 0.7 reduce.4
  326.9 10.5 %gather_fusion = f32[1024]{0:T(1024)} fusion(f32[1536]{0:T(1024)S(1)} %all_to_all.26, s32[1024]{0:T(1024)S(1)} %broadcast_clamp_fusion), kind=kCustom, calls=%fused_computation | custom fusion | bytes 12288 | tf_op jit(solution)/shard_map/gather | solution.py:66
  (43 shorter events, 1.4 us)
Async XLA Ops:
  0.0 12.3 %copy-start = (s32[1024,1]{0,1:T(1,128)S(1)}, s32[1024,1]{0,1:T(1,128)}, u32[]{:S(2)}) copy-start(s32[1024,1]{0,1:T(1,128)} %param.4) | copy-start | bytes 12292
  19.7 49.8 %copy-start.1 = (s32[1024]{0:T(1024)S(1)}, s32[1024]{0:T(1024)}, u32[]{:S(2)}) copy-start(s32[1024]{0:T(1024)} %param.5) | copy-start | bytes 12292
  67.8 72.2 %collective-permute-start.1 = (bf16[1536,1024]{1,0:T(8,128)(2,1)}, bf16[1536,1024]{1,0:T(8,128)(2,1)}, u32[]{:S(2)}, u32[]{:S(2)}) collective-permute-start(bf16[1536,1024]{1,0:T(8,128)(2,1)} %bitcast.7), channel_id=1, source_target_pairs={{0,1},{1,2},{2,3},{3,0},{4,5},{5,6},{6,7},{7,4},{8,9},{9,10},{10,1... | collective-permute-start | bytes 9437192 | tf_op jit(solution)/shard_map/ppermute | solution.py:11
  77.7 62.4 %all-to-all-start = ((bf16[32,48,1]{1,2,0:T(2,128)(2,1)}), bf16[32,48,1]{1,2,0:T(2,128)(2,1)S(1)}, u32[]{:S(2)}, u32[]{:S(2)}) async-start(bf16[32,48,1]{1,2,0:T(2,128)(2,1)} %all_to_all.27), calls=%async_computation | async-start | bytes 32768 | tf_op jit(solution)/shard_map/all_to_all | solution.py:54
  140.0 90.0 %collective-permute-start.3 = (bf16[1536,1024]{1,0:T(8,128)(2,1)}, bf16[1536,1024]{1,0:T(8,128)(2,1)}, u32[]{:S(2)}, u32[]{:S(2)}) collective-permute-start(bf16[1536,1024]{1,0:T(8,128)(2,1)} %collective-permute-done.1), channel_id=1, source_target_pairs={{0,1},{1,2},{2,3},{3,0},{4,5},{5,6},{6,7},{7,4},{8,9},{9,10},{10,1... | collective-permute-start | bytes 9437192 | tf_op jit(solution)/shard_map/ppermute | solution.py:11
  140.2 70.1 %collective-permute-start = (bf16[1536]{0:T(1024)(128)(2,1)S(1)}, bf16[1536]{0:T(1024)(128)(2,1)S(1)}, u32[]{:S(2)}, u32[]{:S(2)}) collective-permute-start(bf16[1536]{0:T(1024)(128)(2,1)S(1)} %eq.82), channel_id=1, source_target_pairs={{0,1},{1,2},{2,3},{3,0},{4,5},{5,6},{6,7},{7,4},{8,9},{9,10},{10,1... | collective-permute-start | bytes 9224 | tf_op jit(solution)/shard_map/ppermute | solution.py:11
  210.3 3.7 %collective-permute-start.2 = (bf16[1536]{0:T(1024)(128)(2,1)S(1)}, bf16[1536]{0:T(1024)(128)(2,1)S(1)}, u32[]{:S(2)}, u32[]{:S(2)}) collective-permute-start(bf16[1536]{0:T(1024)(128)(2,1)S(1)} %collective-permute-done), channel_id=1, source_target_pairs={{0,1},{1,2},{2,3},{3,0},{4,5},{5,6},{6,7},{7,4},{8,9},{9,10},{10,1... | collective-permute-start | bytes 9224 | tf_op jit(solution)/shard_map/ppermute | solution.py:11
  214.0 3.7 %collective-permute-start.4 = (bf16[1536]{0:T(1024)(128)(2,1)S(1)}, bf16[1536]{0:T(1024)(128)(2,1)S(1)}, u32[]{:S(2)}, u32[]{:S(2)}) collective-permute-start(bf16[1536]{0:T(1024)(128)(2,1)S(1)} %collective-permute-done.2), channel_id=1, source_target_pairs={{0,1},{1,2},{2,3},{3,0},{4,5},{5,6},{6,7},{7,4},{8,9},{9,10},{10,1... | collective-permute-start | bytes 9224 | tf_op jit(solution)/shard_map/ppermute | solution.py:11
  230.1 67.0 %collective-permute-start.5 = (bf16[1536,1024]{1,0:T(8,128)(2,1)}, bf16[1536,1024]{1,0:T(8,128)(2,1)S(1)}, u32[]{:S(2)}, u32[]{:S(2)}) collective-permute-start(bf16[1536,1024]{1,0:T(8,128)(2,1)} %collective-permute-done.3), channel_id=1, source_target_pairs={{0,1},{1,2},{2,3},{3,0},{4,5},{5,6},{6,7},{7,4},{8,9},{9,10},{10,1... | collective-permute-start | bytes 9437192 | tf_op jit(solution)/shard_map/ppermute | solution.py:11
  309.5 16.1 %all-to-all-start.2 = ((f32[32,48,1]{1,2,0:T(1,128)}), f32[32,48,1]{1,2,0:T(1,128)S(1)}, u32[]{:S(2)}, u32[]{:S(2)}) async-start(f32[32,48,1]{1,2,0:T(1,128)} %bitcast.8), calls=%async_computation.2 | async-start | bytes 32768 | tf_op jit(solution)/shard_map/all_to_all | solution.py:65
where the time goes:
time: 338 us; the launch traced here: 337 us
  waiting for transfers between devices  184 us (54%)
  matrix products  48.8 us (14%)
  blocking collectives  48.1 us (14%)
  local copies, waits for them, and re-layouts  20.5 us (6%)
  other arithmetic  20.1 us (6%)
  starting transfers between devices  15.7 us (5%)
    ppermute x6, waiting for transfers between devices, shifted(): lax.ppermute(x, axis, [(i, (i + by) % devices) for i in range(devices)])  177 us
    dot_general x12, matrix products, tile_scores(): lax.dot_general(rows, cols[begin:finish], (((1,), (1,)), ((), ())), prefe...  48.8 us
    all_to_all x1, blocking collectives, per_device(): lax.all_to_all(outgoing, 'grp', split_axis=0, concat_axis=0, tiled=True)  48.1 us
    gather x1, local copies, waits for them, and re-layouts, per_device(): return answers[slot]  10.5 us
    all_to_all x1, starting transfers between devices, per_device(): lax.all_to_all(best, 'grp', split_axis=0, concat_axis=0, tiled=True)  9.13 us
    another operation x2, other arithmetic  9.04 us
    scatter x1, local copies, waits for them, and re-layouts, per_device(): out_labels = jnp.full((groups * capacity,), -1.0, jnp.bfloat16).at[slot]....  7.58 us
    scatter x1, other arithmetic, per_device(): jnp.zeros((groups * capacity, width), jnp.bfloat16).at[slot].set(unit)  7.3 us
  transfers between devices with their start and end apart: 8, of which 6 were waited for; matrix products, arithmetic and copies ran while one was open for 13% of the time, Pallas kernels for 0%

commit v1 on v0

v1 whole, which is shorter than its diff:
```python
import functools

import jax
import jax.numpy as jnp
from jax import lax
from jax.experimental import pallas as pl
from jax.experimental.pallas import tpu as pltpu
from jax.sharding import PartitionSpec as P

MESH = pl.DeviceIdType.MESH
F32, BF16, I32 = jnp.float32, jnp.bfloat16, jnp.int32
GROUPS, CAP = 32, 48
HALF = 16 * CAP
LAG = 5
TASKS = 11


def dot_nt(a, b):
    return lax.dot_general(a, b, (((1,), (1,)), ((), ())), preferred_element_type=F32)


def dot_nn(a, b):
    return lax.dot_general(a, b, (((1,), (0,)), ((), ())), preferred_element_type=F32)


def dot_tn(a, b):
    return lax.dot_general(a, b, (((0,), (0,)), ((), ())), preferred_element_type=F32)


def pick(index, values):
    out = values[-1]
    for i in range(len(values) - 2, -1, -1):
        out = jnp.where(index == i, values[i], out)
    return out


def kernel(
    emb_ref, grp_ref, clu_ref, out_ref,
    unit, send, csend, docs, cnts, lab_c, lab_r, sims, row_best, col_best,
    zsend_a, zsend_f, zsend_b, zrecv_a, zrecv_f, zrecv_b, res, ret,
    ss, sr, cs, cr, fs, fr, gs, gr, hs, hr, zs, zr, rs, rr,
):
    g = lax.axis_index("grp")
    z = lax.axis_index("blk")
    y, x, c = g // 8, lax.rem(g // 2, 4), lax.rem(g, 2)
    m = jnp.where(c == 0, z, lax.rem(4 - z, 4))

    def along_z(d):
        return (g, lax.rem(z + jnp.where(c == 0, d, 4 - d), 4))

    def at_offset(k, sign):
        off = lax.rem(7 * k, 32)
        dy, dx, dc = off // 8, lax.rem(off // 2, 4), lax.rem(off, 2)
        ty, tx = lax.rem(y + 4 + sign * dy, 4), lax.rem(x + 4 + sign * dx, 4)
        return ((ty * 4 + tx) * 2 + lax.rem(c + dc, 2), z)

    def remote(src, dst, s_sem, r_sem, target):
        return pltpu.make_async_remote_copy(
            src_ref=src, dst_ref=dst, send_sem=s_sem, recv_sem=r_sem,
            device_id=target, device_id_type=MESH,
        )

    def first_hop(k):
        return remote(send.at[k], docs.at[k], ss.at[k], sr.at[k], at_offset(k, 1))

    def first_counts(k):
        return remote(csend.at[k], cnts.at[k], cs.at[k], cr.at[k], at_offset(k, 1))

    def adjacent(k):
        return remote(docs.at[k], docs.at[32 + k], fs.at[k], fr.at[k], along_z(1))

    def further(k):
        return remote(docs.at[32 + k], docs.at[64 + k], gs.at[k], gr.at[k], along_z(1))

    def back(k):
        return remote(docs.at[k], docs.at[64 + k], gs.at[k], gr.at[k], along_z(3))

    def adjacent_counts(h):
        return remote(
            cnts.at[pl.ds(16 * h, 16)], cnts.at[pl.ds(32 + 16 * h, 16)], hs.at[h], hr.at[h], along_z(1)
        )

    def further_counts():
        return remote(cnts.at[pl.ds(32, 16)], cnts.at[pl.ds(64, 16)], hs.at[2], hr.at[2], along_z(1))

    def back_counts():
        return remote(cnts.at[pl.ds(16, 16)], cnts.at[pl.ds(80, 16)], hs.at[3], hr.at[3], along_z(3))

    sends_further = (m == 1) | (m == 2)
    gets_further = m >= 2
    sends_back = m < 2
    gets_back = (m == 3) | (m == 0)

    zrecv_a[...] = jnp.full_like(zrecv_a, -1.0)
    zrecv_f[...] = jnp.full_like(zrecv_f, -1.0)
    zrecv_b[...] = jnp.full_like(zrecv_b, -1.0)

    barrier = pltpu.get_barrier_semaphore()

    def greet(k, carry):
        pl.semaphore_signal(barrier, 1, device_id=at_offset(k, -1), device_id_type=MESH)
        return carry

    lax.fori_loop(1, 32, greet, 0)
    for d in (1, 2, 3):
        pl.semaphore_signal(barrier, 1, device_id=along_z(d), device_id_type=MESH)

    for b in range(4):
        rows = emb_ref[256 * b : 256 * b + 256, :].astype(F32)
        norm = jnp.sqrt(jnp.sum(rows * rows, axis=1, keepdims=True) + 1e-06)
        unit[256 * b : 256 * b + 256, :] = (rows * (1.0 / norm)).astype(BF16)

    grp = grp_ref[...]
    gy, gx, gc = grp // 8, (grp // 2) & 3, grp & 1
    off = ((gy - y) & 3) * 8 + ((gx - x) & 3) * 2 + ((gc - c) & 1)
    place = (off * 23) & 31
    clu = clu_ref[...]
    kind = place * 2 + clu
    mine = (lax.broadcasted_iota(I32, (64, 1024), 0) == kind).astype(F32)
    mine_b = mine.astype(BF16)
    before = (
        lax.broadcasted_iota(I32, (256, 256), 0) < lax.broadcasted_iota(I32, (256, 256), 1)
    ).astype(F32).astype(BF16)
    offset = jnp.zeros((64, 1), F32)
    ranks = []
    for b in range(4):
        part = mine[:, 256 * b : 256 * b + 256]
        within = dot_nn(mine_b[:, 256 * b : 256 * b + 256], before) + offset
        ranks.append(jnp.sum(part * within, axis=0, keepdims=True))
        offset = offset + jnp.sum(part, axis=1, keepdims=True)
    rank = jnp.concatenate(ranks, axis=1).astype(I32)
    rank = jnp.where(clu == 0, rank, CAP - 1 - rank)
    slot = place * CAP + rank

    same = (lax.broadcasted_iota(I32, (256, 1024), 0) // 4 == kind).astype(F32)
    total = jnp.sum(same, axis=1, keepdims=True)
    csend[...] = jnp.broadcast_to(total, (256, 128)).reshape(32, 8, 128)

    def start_first(k, carry):
        first_hop(k).start()
        first_counts(k).start()
        return carry

    for b in range(4):
        here = lax.broadcasted_iota(I32, (8 * CAP, 1024), 0) + 8 * CAP * b == slot
        picked = dot_nn(here.astype(F32).astype(BF16), unit[...]).astype(BF16)
        send[8 * b : 8 * b + 8] = picked.reshape(8, CAP, 1024)
        if b == 0:
            docs[0] = send[0]
            cnts[0] = csend[0]
            pl.semaphore_wait(barrier, 34)
        lax.fori_loop(max(1, 8 * b), 8 * b + 8, start_first, 0)

    row_best[...] = jnp.full_like(row_best, -1.0)
    col_best[...] = jnp.full_like(col_best, -1.0)

    def relay_further(k):
        adjacent(k).wait_recv()

        @pl.when(sends_further & (k < 16))
        def _():
            further(k).start()

    def relay(k, carry):
        @pl.when(k >= 1)
        def _():
            first_hop(k).wait_recv()
            first_counts(k).wait_recv()

        adjacent(k).start()

        @pl.when(sends_back & (k >= 16))
        def _():
            back(k).start()

        @pl.when(k >= LAG)
        def _():
            relay_further(k - LAG)

        return carry

    def late(k, carry):
        relay_further(k)
        return carry

    def wait_opposite(k, carry):
        further(k).wait_recv()
        return carry

    def prepare(h):
        lane_row = lax.broadcasted_iota(I32, (CAP, 128), 0).astype(F32)
        for k in range(16):
            n0 = cnts[16 * h + k, 0:1, :]
            n1 = cnts[16 * h + k, 4:5, :]
            lab = jnp.where(lane_row < n0, 0.0, jnp.where(lane_row >= CAP - n1, 1.0, -1.0))
            lab_c[HALF * h + CAP * k : HALF * h + CAP * k + CAP, :] = lab
        for b in range(6):
            at = HALF * h + 128 * b
            lab_r[:, at : at + 128] = lab_c[at : at + 128, :].T[0:8, :]

    def step(j, carry):
        lo = pick(j, [0, 16, 23, 28, 32])
        hi = pick(j, [16, 23, 28, 32, 32])
        lax.fori_loop(lo, hi, relay, 0)

        @pl.when(j == 0)
        def _():
            adjacent_counts(0).start()
            prepare(0)

        @pl.when(j == 1)
        def _():
            adjacent_counts(0).wait_recv()

            @pl.when(sends_further)
            def _():
                further_counts().start()

            prepare(2)

        @pl.when((j == 2) & gets_further)
        def _():
            lax.fori_loop(0, 16, wait_opposite, 0)
            further_counts().wait_recv()
            prepare(4)

        @pl.when(j == 3)
        def _():
            adjacent_counts(1).start()

            @pl.when(sends_back)
            def _():
                back_counts().start()

            prepare(1)

        @pl.when(j == 7)
        def _():
            lax.fori_loop(32 - LAG, 32, late, 0)
            adjacent_counts(1).wait_recv()
            prepare(3)

        @pl.when((j == 9) & gets_back)
        def _():
            lax.fori_loop(16, 32, wait_opposite, 0)
            back_counts().wait_recv()
            prepare(5)

        r = pick(j, [0, 0, 0, 0, 1, 1, 1, 0, 1, 2, 3])
        q = pick(j, [0, 2, 4, 1, 1, 2, 4, 3, 3, 5, 5])
        wanted = ((q != 4) | gets_further) & ((q != 5) | gets_back)

        @pl.when(wanted)
        def _():
            left = docs[pl.ds(16 * r, 16)].reshape(HALF, 1024)
            right = docs[pl.ds(16 * q, 16)].reshape(HALF, 1024)
            sims[...] = dot_nt(left, right)

            @pl.when(r == q)
            def _():
                eye = lax.broadcasted_iota(I32, (128, 128), 0) == lax.broadcasted_iota(I32, (128, 128), 1)
                for b in range(6):
                    at = slice(128 * b, 128 * b + 128)
                    sims[at, at] = jnp.where(eye, -1.0, sims[at, at])

            r0 = pl.multiple_of(r * HALF, HALF)
            q0 = pl.multiple_of(q * HALF, HALF)
            labels = lab_c[pl.ds(r0, HALF), :]
            best = row_best[pl.ds(r0, HALF), :]
            for b in range(6):
                tile = sims[:, 128 * b : 128 * b + 128]
                cols = pl.ds(pl.multiple_of(q0 + 128 * b, 128), 128)
                tile = jnp.where(labels == lab_r[0:1, cols], tile, -1.0)
                best = jnp.maximum(best, tile)
                top = jnp.max(tile.reshape(HALF // 8, 8, 128), axis=0)
                col_best[:, cols] = jnp.maximum(col_best[:, cols], top)
            row_best[pl.ds(r0, HALF), :] = best

        return carry

    lax.fori_loop(0, TASKS, step, 0)

    def cols_of(h):
        return jnp.max(col_best[:, HALF * h : HALF * h + HALF], axis=0, keepdims=True)

    def both_of(h):
        parts = []
        for b in range(6):
            at = HALF * h + 128 * b
            parts.append(jnp.max(row_best[at : at + 128, :].T, axis=0, keepdims=True))
        return jnp.maximum(jnp.concatenate(parts, axis=1), cols_of(h))

    to_left = remote(zsend_a, zrecv_a, zs.at[0], zr.at[0], along_z(3))
    to_far = remote(zsend_f, zrecv_f, zs.at[1], zr.at[1], along_z(2))
    to_right = remote(zsend_b, zrecv_b, zs.at[2], zr.at[2], along_z(1))
    zsend_a[:, 0:HALF] = both_of(2)
    zsend_a[:, HALF : 2 * HALF] = both_of(3)
    to_left.start()

    @pl.when(gets_further)
    def _():
        zsend_f[...] = cols_of(4)
        to_far.start()

    @pl.when(gets_back)
    def _():
        zsend_b[...] = cols_of(5)
        to_right.start()

    res[:, 2 * HALF :] = jnp.full((1, 128), -1.0, F32)
    res[:, 0:HALF] = both_of(0)
    res[:, HALF : 2 * HALF] = both_of(1)

    @pl.when(m < 2)
    def _():
        to_far.wait_recv()
        to_right.wait_recv()

    to_left.wait_recv()
    others = jnp.concatenate([zrecv_f[...], zrecv_b[...]], axis=1)
    others = jnp.maximum(others, zrecv_a[...])
    res[:, 0 : 2 * HALF] = jnp.maximum(res[:, 0 : 2 * HALF], others)

    def answer(k):
        at = pl.multiple_of(CAP * k // 128 * 128, 128)
        return remote(res.at[:, pl.ds(at, 256)], ret.at[k], rs.at[k], rr.at[k], at_offset(k, -1))

    def start_answer(k, carry):
        answer(k).start()
        return carry

    lax.fori_loop(1, 32, start_answer, 0)
    ret[0] = res[:, 0:256]

    def sent(k, carry):
        @pl.when(k >= 1)
        def _():
            first_hop(k).wait_send()
            first_counts(k).wait_send()

        adjacent(k).wait_send()

        @pl.when(sends_further & (k < 16))
        def _():
            further(k).wait_send()

        @pl.when(sends_back & (k >= 16))
        def _():
            back(k).wait_send()

        return carry

    lax.fori_loop(0, 32, sent, 0)
    adjacent_counts(0).wait_send()
    adjacent_counts(1).wait_send()
    to_left.wait_send()

    @pl.when(sends_further)
    def _():
        further_counts().wait_send()

    @pl.when(sends_back)
    def _():
        back_counts().wait_send()

    @pl.when(gets_further)
    def _():
        to_far.wait_send()

    @pl.when(gets_back)
    def _():
        to_right.wait_send()

    def answered(k, carry):
        answer(k).wait_recv()
        answer(k).wait_send()
        return carry

    lax.fori_loop(1, 32, answered, 0)
    table = jnp.concatenate([ret[k] for k in range(32)], axis=0)
    where = (lax.broadcasted_iota(I32, (32, 1024), 0) == place).astype(F32).astype(BF16)
    high = table.astype(BF16)
    rest = table - high.astype(F32)
    mid = rest.astype(BF16)
    low = (rest - mid.astype(F32)).astype(BF16)
    found = dot_tn(high, where) + dot_tn(mid, where) + dot_tn(low, where)
    lane = rank + ((place * CAP) & 127)
    hit = lax.broadcasted_iota(I32, (256, 1024), 0) == lane
    out_ref[...] = jnp.max(jnp.where(hit, found, -2.0), axis=0, keepdims=True)


def per_device(embeddings, doc_group, doc_cluster):
    vmem = pl.BlockSpec(memory_space=pltpu.VMEM)
    dma = pltpu.SemaphoreType.DMA
    out = pl.pallas_call(
        kernel,
        out_shape=jax.ShapeDtypeStruct((1, 1024), F32),
        in_specs=[vmem] * 3,
        out_specs=vmem,
        scratch_shapes=[
            pltpu.VMEM((1024, 1024), BF16),
            pltpu.VMEM((32, CAP, 1024), BF16),
            pltpu.VMEM((32, 8, 128), F32),
            pltpu.VMEM((96, CAP, 1024), BF16),
            pltpu.VMEM((96, 8, 128), F32),
            pltpu.VMEM((6 * HALF, 128), F32),
            pltpu.VMEM((8, 6 * HALF), F32),
            pltpu.VMEM((HALF, HALF), F32),
            pltpu.VMEM((4 * HALF, 128), F32),
            pltpu.VMEM((8, 6 * HALF), F32),
            pltpu.VMEM((1, 2 * HALF), F32),
            pltpu.VMEM((1, HALF), F32),
            pltpu.VMEM((1, HALF), F32),
            pltpu.VMEM((1, 2 * HALF), F32),
            pltpu.VMEM((1, HALF), F32),
            pltpu.VMEM((1, HALF), F32),
            pltpu.VMEM((1, 2 * HALF + 128), F32),
            pltpu.VMEM((32, 1, 256), F32),
            dma((32,)), dma((32,)), dma((32,)), dma((32,)),
            dma((32,)), dma((32,)), dma((32,)), dma((32,)),
            dma((4,)), dma((4,)), dma((3,)), dma((3,)), dma((32,)), dma((32,)),
        ],
        compiler_params=pltpu.CompilerParams(
            collective_id=0, has_side_effects=True, vmem_limit_bytes=56 << 20
        ),
        cost_estimate=pl.CostEstimate(flops=24_000_000_000, bytes_accessed=2_200_000, transcendentals=0),
    )(embeddings, doc_group.reshape(1, -1), doc_cluster.reshape(1, -1))
    return out.reshape(-1)


def solution(mesh):
    in_specs = (P(("grp", "blk"), None), P(("grp", "blk"), None), P(("grp", "blk")))
    out_specs = P(("grp", "blk"))
    return jax.shard_map(
        per_device, mesh=mesh, in_specs=in_specs, out_specs=out_specs, check_vma=False
    )
```

time: 338 us -> 98.6 us (0.29)
  waiting for transfers between devices: 184 us -> 0 us
  Pallas kernels: 0 us -> 97.2 us
  matrix products: 48.8 us -> 0 us
  blocking collectives: 48.1 us -> 0 us
  other arithmetic: 20.1 us -> 0 us
  local copies, waits for them, and re-layouts: 20.5 us -> 1.28 us
  starting transfers between devices: 15.7 us -> 0 us
    ppermute x6 -> x0, waiting for transfers between devices: 177 us -> none  [shifted(): lax.ppermute(x, axis, [(i, (i + by) % devices) for i in range(devices)])]
    pallas_call x0 -> x1, Pallas kernels: none -> 97.2 us  [per_device(): pl.pallas_call(kernel, out_shape=jax.ShapeDtypeStruct((1, 1024), F32), in...]
    dot_general x12 -> x0, matrix products: 48.8 us -> none  [tile_scores(): lax.dot_general(rows, cols[begin:finish], (((1,), (1,)), ((), ())), prefe...]
    all_to_all x1 -> x0, blocking collectives: 48.1 us -> none  [per_device(): lax.all_to_all(outgoing, 'grp', split_axis=0, concat_axis=0, tiled=True)]
    all_to_all x2 -> x0, starting transfers between devices: 13.3 us -> none  [the longest x1 9.13 us: per_device(): lax.all_to_all(best, 'grp', split_axis=0, concat_axis=0, tiled=True)]
    gather x1 -> x0, local copies, waits for them, and re-layouts: 10.5 us -> none  [per_device(): return answers[slot]]
    another operation x2 -> x0, other arithmetic: 9.04 us -> none
    scatter x1 -> x0, local copies, waits for them, and re-layouts: 7.58 us -> none  [per_device(): out_labels = jnp.full((groups * capacity,), -1.0, jnp.bfloat16).at[slot]....]
  transfers between devices with their start and end apart: 8 -> 0, of which waited for: 6 -> 0; matrix products, arithmetic and copies ran while one was open for 13% -> 0% of each run, Pallas kernels for 0% -> 0%
where the time goes in v1:
time: 98.6 us; the launch traced here: 98.5 us
  Pallas kernels  97.2 us (99%)
  local copies, waits for them, and re-layouts  1.28 us (1%)
    pallas_call x1, Pallas kernels, per_device(): pl.pallas_call(kernel, out_shape=jax.ShapeDtypeStruct((1, 1024), F32), in...  97.2 us

profile of v1, /device:TPU:1, one launch (start us, length us, event | category | flops | bytes accessed | tf_op | source)
XLA Modules:
  0.0 98.5 jit_solution(1214871583803461091)
XLA Ops:
  0.0 97.2 %shard_map.37 = f32[1,1024]{1,0:T(1,128)} custom-call(bf16[1024,1024]{1,0:T(8,128)(2,1)} %emb_ref.1, s32[1,1024]{1,0:T(1,128)} %bitcast.4, s32[1,1024]{1,0:T(1,128)} %bitcast.5), custom_call_target="tpu_custom_call" | custom-call | flops 24000000000 | bytes 2200000 | tf_op jit(solution)/shard_map/pallas_call | solution.py:395
  97.2 1.3 %copy.5 = f32[1024]{0:T(1024)} copy(f32[1024]{0:T(1024)} %bitcast.3) | data formatting | bytes 8192

commit v2 on v1

v2 whole, which is shorter than its diff:
```python
import functools

import jax
import jax.numpy as jnp
from jax import lax
from jax.experimental import pallas as pl
from jax.experimental.pallas import tpu as pltpu
from jax.sharding import PartitionSpec as P

MESH = pl.DeviceIdType.MESH
F32, BF16, I32 = jnp.float32, jnp.bfloat16, jnp.int32
GROUPS, CAP = 32, 48
HALF = 16 * CAP
LAG = 5
QUARTER = 8 * CAP
TASKS = 22
UNTIL = [16, 17, 19, 21, 24, 25, 28, 30, 32]


def dot_nt(a, b):
    return lax.dot_general(a, b, (((1,), (1,)), ((), ())), preferred_element_type=F32)


def dot_nn(a, b):
    return lax.dot_general(a, b, (((1,), (0,)), ((), ())), preferred_element_type=F32)


def dot_tn(a, b):
    return lax.dot_general(a, b, (((0,), (0,)), ((), ())), preferred_element_type=F32)


def pick(index, values):
    out = values[-1]
    for i in range(len(values) - 2, -1, -1):
        out = jnp.where(index == i, values[i], out)
    return out


def kernel(
    emb_ref, grp_ref, clu_ref, out_ref,
    emb, unit, send, csend, docs, cnts, lab_c, lab_r, sims, row_best, col_best,
    rows_r, zsend_a, zsend_f, zsend_b, zrecv_a, zrecv_f, zrecv_b, res, ret,
    ls, ss, sr, cs, cr, fs, fr, gs, gr, hs, hr, zs, zr, rs, rr,
):
    g = lax.axis_index("grp")
    z = lax.axis_index("blk")
    y, x, c = g // 8, lax.rem(g // 2, 4), lax.rem(g, 2)
    m = jnp.where(c == 0, z, lax.rem(4 - z, 4))

    def along_z(d):
        return (g, lax.rem(z + jnp.where(c == 0, d, 4 - d), 4))

    def at_offset(k, sign):
        off = lax.rem(11 * k, 32)
        dy, dx, dc = off // 8, lax.rem(off // 2, 4), lax.rem(off, 2)
        ty, tx = lax.rem(y + 4 + sign * dy, 4), lax.rem(x + 4 + sign * dx, 4)
        return ((ty * 4 + tx) * 2 + lax.rem(c + dc, 2), z)

    def remote(src, dst, s_sem, r_sem, target):
        return pltpu.make_async_remote_copy(
            src_ref=src, dst_ref=dst, send_sem=s_sem, recv_sem=r_sem,
            device_id=target, device_id_type=MESH,
        )

    def first_hop(k):
        return remote(send.at[k], docs.at[k], ss.at[k], sr.at[k], at_offset(k, 1))

    def first_counts(k):
        return remote(csend.at[k], cnts.at[k], cs.at[k], cr.at[k], at_offset(k, 1))

    def adjacent(k):
        return remote(docs.at[k], docs.at[32 + k], fs.at[k], fr.at[k], along_z(1))

    def further(k):
        return remote(docs.at[32 + k], docs.at[64 + k], gs.at[k], gr.at[k], along_z(1))

    def back(k):
        return remote(docs.at[k], docs.at[64 + k], gs.at[k], gr.at[k], along_z(3))

    def counts(i, to, h, target):
        return remote(cnts.at[pl.ds(8 * i, 8)], cnts.at[pl.ds(8 * to, 8)], hs.at[h], hr.at[h], target)

    def adjacent_counts(i):
        return counts(i, 4 + i, i, along_z(1))

    def further_counts(i):
        return counts(4 + i, 8 + i, 4 + i, along_z(1))

    def back_counts(i):
        return counts(2 + i, 10 + i, 6 + i, along_z(3))

    sends_further = (m == 1) | (m == 2)
    gets_further = m >= 2
    sends_back = m < 2
    gets_back = (m == 3) | (m == 0)

    def load(b):
        at = pl.ds(256 * b, 256)
        return pltpu.make_async_copy(emb_ref.at[at], emb.at[at], ls.at[b])

    for b in range(4):
        load(b).start()

    zrecv_a[...] = jnp.full_like(zrecv_a, -1.0)
    zrecv_f[...] = jnp.full_like(zrecv_f, -1.0)
    zrecv_b[...] = jnp.full_like(zrecv_b, -1.0)

    barrier = pltpu.get_barrier_semaphore()

    def greet(k, carry):
        pl.semaphore_signal(barrier, 1, device_id=at_offset(k, -1), device_id_type=MESH)
        return carry

    lax.fori_loop(1, 32, greet, 0)
    for d in (1, 2, 3):
        pl.semaphore_signal(barrier, 1, device_id=along_z(d), device_id_type=MESH)

    grp = grp_ref[...]
    gy, gx, gc = grp // 8, (grp // 2) & 3, grp & 1
    off = ((gy - y) & 3) * 8 + ((gx - x) & 3) * 2 + ((gc - c) & 1)
    place = (off * 3) & 31
    clu = clu_ref[...]
    kind = place * 2 + clu
    mine = (lax.broadcasted_iota(I32, (64, 1024), 0) == kind).astype(F32)
    mine_b = mine.astype(BF16)
    before = (
        lax.broadcasted_iota(I32, (256, 256), 0) < lax.broadcasted_iota(I32, (256, 256), 1)
    ).astype(F32).astype(BF16)
    offset = jnp.zeros((64, 1), F32)
    ranks = []
    for b in range(4):
        part = mine[:, 256 * b : 256 * b + 256]
        within = dot_nn(mine_b[:, 256 * b : 256 * b + 256], before) + offset
        ranks.append(jnp.sum(part * within, axis=0, keepdims=True))
        offset = offset + jnp.sum(part, axis=1, keepdims=True)
    rank = jnp.concatenate(ranks, axis=1).astype(I32)
    rank = jnp.where(clu == 0, rank, CAP - 1 - rank)
    slot = place * CAP + rank

    same = (lax.broadcasted_iota(I32, (256, 1024), 0) // 4 == kind).astype(F32)
    total = jnp.sum(same, axis=1, keepdims=True)
    csend[...] = jnp.broadcast_to(total, (256, 128)).reshape(32, 8, 128)

    row_best[...] = jnp.full_like(row_best, -1.0)
    col_best[...] = jnp.full_like(col_best, -1.0)

    for b in range(4):
        load(b).wait()
        rows = emb[256 * b : 256 * b + 256, :].astype(F32)
        norm = jnp.sqrt(jnp.sum(rows * rows, axis=1, keepdims=True) + 1e-06)
        unit[256 * b : 256 * b + 256, :] = (rows * (1.0 / norm)).astype(BF16)

    def start_first(k, carry):
        first_hop(k).start()
        first_counts(k).start()
        return carry

    for b in range(4):
        here = lax.broadcasted_iota(I32, (8 * CAP, 1024), 0) + 8 * CAP * b == slot
        picked = dot_nn(here.astype(F32).astype(BF16), unit[...]).astype(BF16)
        send[8 * b : 8 * b + 8] = picked.reshape(8, CAP, 1024)
        if b == 0:
            docs[0] = send[0]
            cnts[0] = csend[0]
            pl.semaphore_wait(barrier, 34)
        lax.fori_loop(max(1, 8 * b), 8 * b + 8, start_first, 0)

    def relay_further(k):
        adjacent(k).wait_recv()

        @pl.when(sends_further & (k < 16))
        def _():
            further(k).start()

    def relay(k, carry):
        @pl.when(k >= 1)
        def _():
            first_hop(k).wait_recv()
            first_counts(k).wait_recv()

        adjacent(k).start()

        @pl.when(sends_back & (k >= 16))
        def _():
            back(k).start()

        @pl.when(lax.rem(k, 8) == 7)
        def _():
            adjacent_counts(k // 8).start()

            @pl.when(sends_back & (k >= 16))
            def _():
                back_counts(k // 8 - 2).start()

        @pl.when(k >= LAG)
        def _():
            relay_further(k - LAG)

        return carry

    def late(k, carry):
        relay_further(k)
        return carry

    def wait_opposite(k, carry):
        further(k).wait_recv()
        return carry

    def prepare(r):
        lane_row = lax.broadcasted_iota(I32, (CAP, 128), 0).astype(F32)
        for k in range(8):
            n0 = cnts[8 * r + k, 0:1, :]
            n1 = cnts[8 * r + k, 4:5, :]
            lab = jnp.where(lane_row < n0, 0.0, jnp.where(lane_row >= CAP - n1, 1.0, -1.0))
            at = QUARTER * r + CAP * k
            lab_c[at : at + CAP, :] = lab
        if r < 8:
            for b in range(3):
                at = QUARTER * r + 128 * b
                lab_r[:, at : at + 128] = lab_c[at : at + 128, :].T[0:8, :]

    def lanes_of(r):
        for b in range(3):
            at = QUARTER * r + 128 * b
            rows_r[:, at : at + 128] = jnp.max(row_best[at : at + 128, :].T, axis=0, keepdims=True)

    def step(j, carry):
        lo, hi = pick(j, [0] + UNTIL), pick(j, UNTIL + [32])
        lax.fori_loop(lo, hi, relay, 0)

        def before(i, only=None):
            return pl.when(j == i if only is None else (j == i) & only)

        @before(0)
        def _():
            prepare(0)
            prepare(1)

        for i in (0, 1):

            @before(2 + i)
            def _(i=i):
                adjacent_counts(i).wait_recv()

                @pl.when(sends_further)
                def _():
                    further_counts(i).start()

                prepare(4 + i)

            @before((4, 6)[i], gets_further)
            def _(i=i):
                further_counts(i).wait_recv()
                lax.fori_loop(8 * i, 8 * i + 8, wait_opposite, 0)
                prepare(8 + i)

            @before((8, 20)[i], gets_back)
            def _(i=i):
                back_counts(i).wait_recv()
                lax.fori_loop(16 + 8 * i, 24 + 8 * i, wait_opposite, 0)
                prepare(10 + i)

        @before(5)
        def _():
            prepare(2)

        @before(7)
        def _():
            adjacent_counts(2).wait_recv()
            prepare(6)

        @before(9)
        def _():
            prepare(3)

        @before(17)
        def _():
            for r in range(7):
                lanes_of(r)

            @pl.when(gets_further)
            def _():
                for r in (8, 9):
                    lanes_of(r)
                zsend_f[...] = rows_r[:, 4 * HALF : 5 * HALF]
                to_far.start()

            lax.fori_loop(32 - LAG, 32, late, 0)
            adjacent_counts(3).wait_recv()
            prepare(7)

        r = pick(j, [0, 1, 4, 5, 8, 2, 9, 6, 10, 3, 2, 3, 4, 5, 8, 9, 6, 7, 7, 10, 11, 11])
        q = pick(j, [0, 0, 0, 0, 0, 0, 0, 0, 2, 0, 1, 1, 1, 1, 1, 1, 1, 0, 1, 3, 2, 3])
        wanted = (r < 8) | ((r < 10) & gets_further) | ((r >= 10) & gets_back)

        @pl.when(wanted)
        def _():
            left = docs[pl.ds(8 * r, 8)].reshape(QUARTER, 1024)
            right = docs[pl.ds(16 * q, 16)].reshape(HALF, 1024)
            sims[...] = dot_nt(left, right)

            @pl.when(r // 2 == q)
            def _():
                eye = lax.broadcasted_iota(I32, (128, 128), 0) == lax.broadcasted_iota(I32, (128, 128), 1)
                for b in range(3):
                    at = slice(128 * b, 128 * b + 128)
                    to = pl.ds(pl.multiple_of(QUARTER * lax.rem(r, 2) + 128 * b, 128), 128)
                    sims[at, to] = jnp.where(eye, -1.0, sims[at, to])

            r0 = pl.multiple_of(r * QUARTER, QUARTER)
            q0 = pl.multiple_of(q * HALF, HALF)
            labels = lab_c[pl.ds(r0, QUARTER), :]
            best = row_best[pl.ds(r0, QUARTER), :]
            for b in range(6):
                tile = sims[:, 128 * b : 128 * b + 128]
                cols = pl.ds(pl.multiple_of(q0 + 128 * b, 128), 128)
                tile = jnp.where(labels == lab_r[0:1, cols], tile, -1.0)
                best = jnp.maximum(best, tile)
                top = jnp.max(tile.reshape(QUARTER // 8, 8, 128), axis=0)
                col_best[:, cols] = jnp.maximum(col_best[:, cols], top)
            row_best[pl.ds(r0, QUARTER), :] = best

        return carry

    to_left = remote(zsend_a, zrecv_a, zs.at[0], zr.at[0], along_z(3))
    to_far = remote(zsend_f, zrecv_f, zs.at[1], zr.at[1], along_z(2))
    to_right = remote(zsend_b, zrecv_b, zs.at[2], zr.at[2], along_z(1))
    lax.fori_loop(0, TASKS, step, 0)

    def cols_of(h):
        return jnp.max(col_best[:, HALF * h : HALF * h + HALF], axis=0, keepdims=True)

    def both_of(h):
        return jnp.maximum(rows_r[:, HALF * h : HALF * h + HALF], cols_of(h))

    lanes_of(7)
    zsend_a[:, 0:HALF] = both_of(2)
    zsend_a[:, HALF : 2 * HALF] = both_of(3)
    to_left.start()

    @pl.when(gets_back)
    def _():
        lanes_of(10)
        lanes_of(11)
        zsend_b[...] = rows_r[:, 5 * HALF : 6 * HALF]
        to_right.start()

    res[:, 2 * HALF :] = jnp.full((1, 128), -1.0, F32)
    res[:, 0:HALF] = both_of(0)
    res[:, HALF : 2 * HALF] = both_of(1)

    @pl.when(m < 2)
    def _():
        to_far.wait_recv()
        to_right.wait_recv()

    to_left.wait_recv()
    others = jnp.concatenate([zrecv_f[...], zrecv_b[...]], axis=1)
    others = jnp.maximum(others, zrecv_a[...])
    res[:, 0 : 2 * HALF] = jnp.maximum(res[:, 0 : 2 * HALF], others)

    def answer(k):
        at = CAP * k // 128 * 128
        return remote(res.at[:, pl.ds(at, 256)], ret.at[k], rs.at[k], rr.at[k], at_offset(k, -1))

    for k in range(1, 32):
        answer(k).start()
    ret[0] = res[:, 0:256]

    def sent(k, carry):
        @pl.when(k >= 1)
        def _():
            first_hop(k).wait_send()
            first_counts(k).wait_send()

        adjacent(k).wait_send()

        @pl.when(sends_further & (k < 16))
        def _():
            further(k).wait_send()

        @pl.when(sends_back & (k >= 16))
        def _():
            back(k).wait_send()

        return carry

    lax.fori_loop(0, 32, sent, 0)
    for i in range(4):
        adjacent_counts(i).wait_send()
    to_left.wait_send()

    @pl.when(sends_further)
    def _():
        for i in (0, 1):
            further_counts(i).wait_send()

    @pl.when(sends_back)
    def _():
        for i in (0, 1):
            back_counts(i).wait_send()

    @pl.when(gets_further)
    def _():
        to_far.wait_send()

    @pl.when(gets_back)
    def _():
        to_right.wait_send()

    for k in range(1, 32):
        answer(k).wait_recv()
        answer(k).wait_send()
    table = jnp.concatenate([ret[k] for k in range(32)], axis=0)
    where = (lax.broadcasted_iota(I32, (32, 1024), 0) == place).astype(F32).astype(BF16)
    high = table.astype(BF16)
    rest = table - high.astype(F32)
    mid = rest.astype(BF16)
    low = (rest - mid.astype(F32)).astype(BF16)
    found = dot_tn(high, where) + dot_tn(mid, where) + dot_tn(low, where)
    lane = rank + ((place * CAP) & 127)
    hit = lax.broadcasted_iota(I32, (256, 1024), 0) == lane
    out_ref[...] = jnp.max(jnp.where(hit, found, -2.0), axis=0, keepdims=True)


def per_device(embeddings, doc_group, doc_cluster):
    vmem = pl.BlockSpec(memory_space=pltpu.VMEM)
    dma = pltpu.SemaphoreType.DMA
    out = pl.pallas_call(
        kernel,
        out_shape=jax.ShapeDtypeStruct((1, 1024), F32),
        in_specs=[pl.BlockSpec(memory_space=pl.ANY), vmem, vmem],
        out_specs=vmem,
        scratch_shapes=[
            pltpu.VMEM((1024, 1024), BF16),
            pltpu.VMEM((1024, 1024), BF16),
            pltpu.VMEM((32, CAP, 1024), BF16),
            pltpu.VMEM((32, 8, 128), F32),
            pltpu.VMEM((96, CAP, 1024), BF16),
            pltpu.VMEM((96, 8, 128), F32),
            pltpu.VMEM((6 * HALF, 128), F32),
            pltpu.VMEM((8, 4 * HALF), F32),
            pltpu.VMEM((QUARTER, HALF), F32),
            pltpu.VMEM((6 * HALF, 128), F32),
            pltpu.VMEM((8, 4 * HALF), F32),
            pltpu.VMEM((1, 6 * HALF), F32),
            pltpu.VMEM((1, 2 * HALF), F32),
            pltpu.VMEM((1, HALF), F32),
            pltpu.VMEM((1, HALF), F32),
            pltpu.VMEM((1, 2 * HALF), F32),
            pltpu.VMEM((1, HALF), F32),
            pltpu.VMEM((1, HALF), F32),
            pltpu.VMEM((1, 2 * HALF + 128), F32),
            pltpu.VMEM((32, 1, 256), F32),
            dma((4,)), dma((32,)), dma((32,)), dma((32,)), dma((32,)),
            dma((32,)), dma((32,)), dma((32,)), dma((32,)),
            dma((8,)), dma((8,)), dma((3,)), dma((3,)), dma((32,)), dma((32,)),
        ],
        compiler_params=pltpu.CompilerParams(
            collective_id=0, has_side_effects=True, vmem_limit_bytes=56 << 20
        ),
        cost_estimate=pl.CostEstimate(flops=24_000_000_000, bytes_accessed=2_200_000, transcendentals=0),
    )(embeddings, doc_group.reshape(1, -1), doc_cluster.reshape(1, -1))
    return out.reshape(-1)


def solution(mesh):
    in_specs = (P(("grp", "blk"), None), P(("grp", "blk"), None), P(("grp", "blk")))
    out_specs = P(("grp", "blk"))
    return jax.shard_map(
        per_device, mesh=mesh, in_specs=in_specs, out_specs=out_specs, check_vma=False
    )
```

time: 98.6 us -> 97 us (0.984)
  Pallas kernels: 97.2 us -> 95.5 us
    pallas_call x1, Pallas kernels: 97.2 us -> 95.5 us  [per_device(): pl.pallas_call(kernel, out_shape=jax.ShapeDtypeStruct((1, 1024), F32), in...]
where the time goes in v2:
time: 97 us; the launch traced here: 96.8 us
  Pallas kernels  95.5 us (98%)
  local copies, waits for them, and re-layouts  1.28 us (1%)
    pallas_call x1, Pallas kernels, per_device(): pl.pallas_call(kernel, out_shape=jax.ShapeDtypeStruct((1, 1024), F32), in...  95.5 us

profile of v2, /device:TPU:1, one launch (start us, length us, event | category | flops | bytes accessed | tf_op | source)
XLA Modules:
  0.0 96.8 jit_solution(10244953826401791502)
XLA Ops:
  0.0 95.5 %shard_map.37 = f32[1,1024]{1,0:T(1,128)} custom-call(bf16[1024,1024]{1,0:T(8,128)(2,1)} %emb_ref.1, s32[1,1024]{1,0:T(1,128)} %bitcast.4, s32[1,1024]{1,0:T(1,128)} %bitcast.5), custom_call_target="tpu_custom_call" | custom-call | flops 24000000000 | bytes 2200000 | tf_op jit(solution)/shard_map/pallas_call | solution.py:429
  95.5 1.3 %copy.5 = f32[1024]{0:T(1024)} copy(f32[1024]{0:T(1024)} %bitcast.3) | data formatting | bytes 8192

commit v3 on v2

--- a/solution.py
+++ b/solution.py
@@ -11,10 +11,20 @@
 F32, BF16, I32 = jnp.float32, jnp.bfloat16, jnp.int32
 GROUPS, CAP = 32, 48
 HALF = 16 * CAP
-LAG = 5
+LAG = 7
 QUARTER = 8 * CAP
-TASKS = 22
-UNTIL = [16, 17, 19, 21, 24, 25, 28, 30, 32]
+ORDER = [
+    (0, 0, 16), (1, 0, 17), (4, 0, 19), (5, 0, 23), (8, 0, 24), (2, 0, 25),
+    (9, 0, 27), (6, 0, 31), (10, 2, 32), (3, 0, 32), (2, 1, 32), (3, 1, 32),
+    (4, 1, 32), (5, 1, 32), (8, 1, 32), (9, 1, 32), (6, 1, 32), (7, 0, 32),
+    (7, 1, 32), (10, 3, 32), (11, 2, 32), (11, 3, 32),
+]
+TASKS = len(ORDER)
+OFFSETS = [
+    0, 1, 6, 30, 18, 2, 8, 7, 31, 19, 3, 9, 12, 14, 16, 26,
+    4, 13, 15, 17, 27, 5, 24, 10, 20, 28, 22, 25, 11, 21, 29, 23,
+]
+AT = {(r, q): j for j, (r, q, _) in reversed(list(enumerate(ORDER)))}
 
 
 def dot_nt(a, b):
@@ -51,8 +61,8 @@
         return (g, lax.rem(z + jnp.where(c == 0, d, 4 - d), 4))
 
     def at_offset(k, sign):
-        off = lax.rem(11 * k, 32)
-        dy, dx, dc = off // 8, lax.rem(off // 2, 4), lax.rem(off, 2)
+        off = OFFSETS[k]
+        dy, dx, dc = off // 8, off // 2 % 4, off % 2
         ty, tx = lax.rem(y + 4 + sign * dy, 4), lax.rem(x + 4 + sign * dx, 4)
         return ((ty * 4 + tx) * 2 + lax.rem(c + dc, 2), z)
 
@@ -63,10 +73,12 @@
         )
 
     def first_hop(k):
-        return remote(send.at[k], docs.at[k], ss.at[k], sr.at[k], at_offset(k, 1))
+        to = at_offset(k, 1) if isinstance(k, int) else along_z(1)
+        return remote(send.at[k], docs.at[k], ss.at[k], sr.at[k], to)
 
     def first_counts(k):
-        return remote(csend.at[k], cnts.at[k], cs.at[k], cr.at[k], at_offset(k, 1))
+        to = at_offset(k, 1) if isinstance(k, int) else along_z(1)
+        return remote(csend.at[k], cnts.at[k], cs.at[k], cr.at[k], to)
 
     def adjacent(k):
         return remote(docs.at[k], docs.at[32 + k], fs.at[k], fr.at[k], along_z(1))
@@ -111,14 +123,17 @@
         pl.semaphore_signal(barrier, 1, device_id=at_offset(k, -1), device_id_type=MESH)
         return carry
 
-    lax.fori_loop(1, 32, greet, 0)
+    for k in range(1, 32):
+        greet(k, 0)
     for d in (1, 2, 3):
         pl.semaphore_signal(barrier, 1, device_id=along_z(d), device_id_type=MESH)
 
     grp = grp_ref[...]
     gy, gx, gc = grp // 8, (grp // 2) & 3, grp & 1
     off = ((gy - y) & 3) * 8 + ((gx - x) & 3) * 2 + ((gc - c) & 1)
-    place = (off * 3) & 31
+    place = jnp.zeros_like(off)
+    for k in range(1, 32):
+        place = jnp.where(off == OFFSETS[k], k, place)
     clu = clu_ref[...]
     kind = place * 2 + clu
     mine = (lax.broadcasted_iota(I32, (64, 1024), 0) == kind).astype(F32)
@@ -150,11 +165,6 @@
         norm = jnp.sqrt(jnp.sum(rows * rows, axis=1, keepdims=True) + 1e-06)
         unit[256 * b : 256 * b + 256, :] = (rows * (1.0 / norm)).astype(BF16)
 
-    def start_first(k, carry):
-        first_hop(k).start()
-        first_counts(k).start()
-        return carry
-
     for b in range(4):
         here = lax.broadcasted_iota(I32, (8 * CAP, 1024), 0) + 8 * CAP * b == slot
         picked = dot_nn(here.astype(F32).astype(BF16), unit[...]).astype(BF16)
@@ -163,7 +173,9 @@
             docs[0] = send[0]
             cnts[0] = csend[0]
             pl.semaphore_wait(barrier, 34)
-        lax.fori_loop(max(1, 8 * b), 8 * b + 8, start_first, 0)
+        for k in range(max(1, 8 * b), 8 * b + 8):
+            first_hop(k).start()
+            first_counts(k).start()
 
     def relay_further(k):
         adjacent(k).wait_recv()
@@ -192,7 +204,7 @@
             def _():
                 back_counts(k // 8 - 2).start()
 
-        @pl.when(k >= LAG)
+        @pl.when((k >= LAG) & (k < LAG + 16))
         def _():
             relay_further(k - LAG)
 
@@ -225,20 +237,20 @@
             rows_r[:, at : at + 128] = jnp.max(row_best[at : at + 128, :].T, axis=0, keepdims=True)
 
     def step(j, carry):
-        lo, hi = pick(j, [0] + UNTIL), pick(j, UNTIL + [32])
-        lax.fori_loop(lo, hi, relay, 0)
+        until = [u for _, _, u in ORDER]
+        lax.fori_loop(pick(j, [0] + until[:-1]), pick(j, until), relay, 0)
 
         def before(i, only=None):
             return pl.when(j == i if only is None else (j == i) & only)
 
-        @before(0)
+        @before(AT[0, 0])
         def _():
             prepare(0)
             prepare(1)
 
         for i in (0, 1):
 
-            @before(2 + i)
+            @before(AT[4 + i, 0])
             def _(i=i):
                 adjacent_counts(i).wait_recv()
 
@@ -248,32 +260,33 @@
 
                 prepare(4 + i)
 
-            @before((4, 6)[i], gets_further)
+            @before(AT[8 + i, 0], gets_further)
             def _(i=i):
                 further_counts(i).wait_recv()
                 lax.fori_loop(8 * i, 8 * i + 8, wait_opposite, 0)
                 prepare(8 + i)
 
-            @before((8, 20)[i], gets_back)
+            @before(AT[10 + i, 2], gets_back)
             def _(i=i):
                 back_counts(i).wait_recv()
                 lax.fori_loop(16 + 8 * i, 24 + 8 * i, wait_opposite, 0)
                 prepare(10 + i)
 
-        @before(5)
+        @before(AT[2, 0])
         def _():
             prepare(2)
 
-        @before(7)
-        def _():
+        @before(AT[6, 0])
+        def _():
+            lax.fori_loop(16, 24, late, 0)
             adjacent_counts(2).wait_recv()
             prepare(6)
 
-        @before(9)
+        @before(AT[3, 0])
         def _():
             prepare(3)
 
-        @before(17)
+        @before(AT[7, 0])
         def _():
             for r in range(7):
                 lanes_of(r)
@@ -285,12 +298,12 @@
                 zsend_f[...] = rows_r[:, 4 * HALF : 5 * HALF]
                 to_far.start()
 
-            lax.fori_loop(32 - LAG, 32, late, 0)
+            lax.fori_loop(24, 32, late, 0)
             adjacent_counts(3).wait_recv()
             prepare(7)
 
-        r = pick(j, [0, 1, 4, 5, 8, 2, 9, 6, 10, 3, 2, 3, 4, 5, 8, 9, 6, 7, 7, 10, 11, 11])
-        q = pick(j, [0, 0, 0, 0, 0, 0, 0, 0, 2, 0, 1, 1, 1, 1, 1, 1, 1, 0, 1, 3, 2, 3])
+        r = pick(j, [r for r, _, _ in ORDER])
+        q = pick(j, [q for _, q, _ in ORDER])
         wanted = (r < 8) | ((r < 10) & gets_further) | ((r >= 10) & gets_back)
 
         @pl.when(wanted)

time: 97 us -> 93.8 us (0.967)
  Pallas kernels: 95.5 us -> 92.3 us
    pallas_call x1, Pallas kernels: 95.5 us -> 92.3 us  [per_device(): pl.pallas_call(kernel, out_shape=jax.ShapeDtypeStruct((1, 1024), F32), in...]
where the time goes in v3:
time: 93.8 us; the launch traced here: 93.6 us
  Pallas kernels  92.3 us (98%)
  local copies, waits for them, and re-layouts  1.28 us (1%)
    pallas_call x1, Pallas kernels, per_device(): pl.pallas_call(kernel, out_shape=jax.ShapeDtypeStruct((1, 1024), F32), in...  92.3 us

profile of v3, /device:TPU:1, one launch (start us, length us, event | category | flops | bytes accessed | tf_op | source)
XLA Modules:
  0.0 93.6 jit_solution(526187091438815129)
XLA Ops:
  0.0 92.3 %shard_map.37 = f32[1,1024]{1,0:T(1,128)} custom-call(bf16[1024,1024]{1,0:T(8,128)(2,1)} %emb_ref.1, s32[1,1024]{1,0:T(1,128)} %bitcast.4, s32[1,1024]{1,0:T(1,128)} %bitcast.5), custom_call_target="tpu_custom_call" | custom-call | flops 24000000000 | bytes 2200000 | tf_op jit(solution)/shard_map/pallas_call | solution.py:442
  92.3 1.3 %copy.5 = f32[1024]{0:T(1024)} copy(f32[1024]{0:T(1024)} %bitcast.3) | data formatting | bytes 8192
